TPU v7x, 32 devices: a whole 2x2x4 slice. The times are simulated.
32 devices in a mesh: dp: 8 (over z, y), tensor: 4 (over x, core).
Axes of the slice: x: 2, y: 2, z: 4, core: 2. Of those that a mesh axis runs over, the one named last changes fastest.
Arguments:
- tokens: bfloat16 [8192, 768], P('dp'), may hold values from -6 to 6
- text_states: bfloat16 [32, 77, 768], P('dp'), may hold values from -6 to 6
- clip_len: int32 [32], P('dp'), may hold values from 0 to 1024, as said below
- text_len: int32 [32], P('dp'), may hold values from 1 to 77
- timesteps: int32 [32], P('dp'), may hold values from 0 to 999
- q_weight: bfloat16 [768, 768], P(None, 'tensor'), may hold values from -0.21875 to 0.21875
- k_weight: bfloat16 [768, 768], P(None, 'tensor'), may hold values from -0.21875 to 0.21875
- v_weight: bfloat16 [768, 768], P(None, 'tensor'), may hold values from -0.21875 to 0.21875
- o_weight: bfloat16 [768, 768], P('tensor'), may hold values from -3 to 3
- cross_q: bfloat16 [768, 768], P(None, 'tensor'), may hold values from -0.21875 to 0.21875
- cross_k: bfloat16 [768, 768], P(None, 'tensor'), may hold values from -0.21875 to 0.21875
- cross_v: bfloat16 [768, 768], P(None, 'tensor'), may hold values from -0.21875 to 0.21875
- cross_o: bfloat16 [768, 768], P('tensor'), may hold values from -1.25 to 1.25
- mlp_in: bfloat16 [768, 3072], P(None, 'tensor'), may hold values from -0.3125 to 0.3125
- mlp_out: bfloat16 [3072, 768], P('tensor'), may hold values from -0.21875 to 0.21875
- mod_weight: bfloat16 [768, 6912], P(None, 'tensor'), may hold values from -0.21875 to 0.21875
- mod_bias: bfloat16 [6912], P('tensor'), may hold values from -3 to 3
- cotangent: bfloat16 [8192, 768], P('dp'), may hold values from -6 to 6
Outputs:
- mixed: bfloat16 [8192, 768], P('dp')
- token_grad: bfloat16 [8192, 768], P('dp')
- q_weight_grad: float32 [768, 768], P(None, 'tensor')
- k_weight_grad: float32 [768, 768], P(None, 'tensor')
- v_weight_grad: float32 [768, 768], P(None, 'tensor')
- o_weight_grad: float32 [768, 768], P('tensor')
- cross_q_grad: float32 [768, 768], P(None, 'tensor')
- cross_k_grad: float32 [768, 768], P(None, 'tensor')
- cross_v_grad: float32 [768, 768], P(None, 'tensor')
- cross_o_grad: float32 [768, 768], P('tensor')
- mlp_in_grad: float32 [768, 3072], P(None, 'tensor')
- mlp_out_grad: float32 [3072, 768], P('tensor')
- mod_weight_grad: float32 [768, 6912], P(None, 'tensor')
- mod_bias_grad: float32 [6912], P('tensor')
Inputs may be any that keep to these rules, and one draw needn't show every extreme that they name: `clip_len`: each aligned run of 4 entries lists, in order, clip lengths of 256, 512 or 1024 frames that sum to 1024, followed by zeros for unused slots.
All inputs are finite; a program needn't handle non-finite values.
Results may differ from a plain program's by a relative error of at most 0.028.
Values may be sent and summed in bfloat16 or wider, within the bound.
No kernel may reach another device: no remote copies, remote signals or barrier semaphores. Data moves between devices by JAX's collectives and lax.ppermute only.
A program may use at most 192 MiB of HBM per device.

v0:
```python
import math

import jax
import jax.numpy as jnp
from jax import lax
from jax.sharding import PartitionSpec as P

D = 768
HEADS = 12


epsilon = 1e-06
masked_score = -1000000000.0


def matmul(left_side, right_side):
    return jnp.dot(left_side, right_side, preferred_element_type=jnp.float32)


def matmul_tn(left_side, right_side):
    return lax.dot_general(
        left_side, right_side, (((0,), (0,)), ((), ())), preferred_element_type=jnp.float32
    )


def matmul_nt(left_side, right_side):
    return lax.dot_general(
        left_side, right_side, (((1,), (1,)), ((), ())), preferred_element_type=jnp.float32
    )


def exact_tn(left_side, right_side):
    return lax.dot_general(
        left_side,
        right_side,
        (((0,), (0,)), ((), ())),
        precision=lax.Precision.HIGHEST,
        preferred_element_type=jnp.float32,
    )


def sinusoid(step_ids, model_width):
    half_width = model_width // 2
    ramp_index = jnp.arange(half_width).astype(jnp.float32)
    frequency = jnp.exp(ramp_index * (-math.log(10000.0) / half_width))
    angles = step_ids.astype(jnp.float32)[:, None] * frequency[None, :]
    return jnp.concatenate([jnp.cos(angles), jnp.sin(angles)], axis=1)


def normalize(values):
    row_mean = jnp.mean(values, axis=-1, keepdims=True)
    centered = values - row_mean
    variance = jnp.mean(centered * centered, axis=-1, keepdims=True)
    inverse = lax.rsqrt(variance + epsilon)
    return (centered * inverse, inverse)


def norm_back(grad_normed, normed, inverse):
    first_mean = jnp.mean(grad_normed, axis=-1, keepdims=True)
    second_mean = jnp.mean(grad_normed * normed, axis=-1, keepdims=True)
    return inverse * (grad_normed - first_mean - normed * second_mean)


def attend_forward(queries, key_rows, value_rows, allowed, score_scale):
    head_dim = D // HEADS
    row_count = queries.shape[0]
    head_count = queries.shape[1] // head_dim
    block_rows = min(512, row_count)
    query_heads = queries.reshape(row_count, head_count, head_dim)
    key_heads = key_rows.reshape(key_rows.shape[0], head_count, head_dim)
    value_heads = value_rows.reshape(value_rows.shape[0], head_count, head_dim)
    outputs = []
    log_sums = []
    for offset in range(0, row_count, block_rows):
        scores = (
            jnp.einsum(
                "qhd,khd->hqk",
                query_heads[offset : offset + block_rows],
                key_heads,
                preferred_element_type=jnp.float32,
            )
            * score_scale
        )
        scores = jnp.where(allowed[offset : offset + block_rows][None], scores, masked_score)
        row_max = jnp.max(scores, axis=-1, keepdims=True)
        raised = jnp.exp(scores - row_max)
        row_total = jnp.sum(raised, axis=-1, keepdims=True)
        weights_low = (raised / row_total).astype(jnp.bfloat16)
        block_out = jnp.einsum(
            "hqk,khd->qhd", weights_low, value_heads, preferred_element_type=jnp.float32
        )
        outputs.append(block_out.reshape(block_rows, head_count * head_dim))
        log_sums.append(row_max[..., 0] + jnp.log(row_total[..., 0]))
    return (jnp.concatenate(outputs, axis=0), jnp.concatenate(log_sums, axis=1))


def attend_backward(queries, key_rows, value_rows, allowed, score_scale, log_sums, out_grad):
    head_dim = D // HEADS
    row_count = queries.shape[0]
    head_count = queries.shape[1] // head_dim
    block_rows = min(512, row_count)
    query_heads = queries.reshape(row_count, head_count, head_dim)
    key_heads = key_rows.reshape(key_rows.shape[0], head_count, head_dim)
    value_heads = value_rows.reshape(value_rows.shape[0], head_count, head_dim)
    grad_heads = out_grad.reshape(row_count, head_count, head_dim)
    key_grad = jnp.zeros(key_heads.shape, jnp.float32)
    value_grad = jnp.zeros(value_heads.shape, jnp.float32)
    query_grads = []
    for offset in range(0, row_count, block_rows):
        query_block = query_heads[offset : offset + block_rows]
        grad_block = grad_heads[offset : offset + block_rows]
        scores = (
            jnp.einsum("qhd,khd->hqk", query_block, key_heads, preferred_element_type=jnp.float32)
            * score_scale
        )
        scores = jnp.where(allowed[offset : offset + block_rows][None], scores, masked_score)
        probabilities = jnp.exp(scores - log_sums[:, offset : offset + block_rows][..., None])
        prob_grad = jnp.einsum(
            "qhd,khd->hqk", grad_block, value_heads, preferred_element_type=jnp.float32
        )
        value_grad = value_grad + jnp.einsum(
            "hqk,qhd->khd",
            probabilities.astype(jnp.bfloat16),
            grad_block,
            preferred_element_type=jnp.float32,
        )
        row_dot = jnp.sum(probabilities * prob_grad, axis=-1, keepdims=True)
        score_grad = (probabilities * (prob_grad - row_dot)).astype(jnp.bfloat16)
        query_block_grad = jnp.einsum(
            "hqk,khd->qhd", score_grad, key_heads, preferred_element_type=jnp.float32
        )
        query_grads.append(
            (query_block_grad * score_scale).reshape(block_rows, head_count * head_dim)
        )
        key_grad = (
            key_grad
            + jnp.einsum(
                "hqk,qhd->khd", score_grad, query_block, preferred_element_type=jnp.float32
            )
            * score_scale
        )
    return (
        jnp.concatenate(query_grads, axis=0),
        key_grad.reshape(key_rows.shape[0], head_count * head_dim),
        value_grad.reshape(value_rows.shape[0], head_count * head_dim),
    )


def local(
    tokens,
    text_states,
    clip_len,
    text_len,
    timesteps,
    q_weight,
    k_weight,
    v_weight,
    o_weight,
    cross_q,
    cross_k,
    cross_v,
    cross_o,
    mlp_in,
    mlp_out,
    mod_weight,
    mod_bias,
    cotangent,
):
    row_count = tokens.shape[0]
    model_width = tokens.shape[1]
    slot_count = clip_len.shape[0]
    text_rows = text_states.shape[1]
    score_scale = float(D // HEADS) ** (-0.5)
    clip_ends = jnp.cumsum(clip_len)
    position = jnp.arange(row_count, dtype=jnp.int32)
    clip_index = jnp.sum((position[:, None] >= clip_ends[None, :]).astype(jnp.int32), axis=1)
    onehot = (clip_index[:, None] == jnp.arange(slot_count, dtype=jnp.int32)[None, :]).astype(
        jnp.float32
    )
    self_allowed = clip_index[:, None] == clip_index[None, :]
    key_range = jnp.arange(slot_count * text_rows, dtype=jnp.int32)
    key_slot = key_range // text_rows
    key_place = key_range % text_rows
    key_limit = jnp.repeat(text_len, text_rows)
    cross_allowed = (clip_index[:, None] == key_slot[None, :]) & (key_place < key_limit)[None, :]
    silu_low = jax.nn.silu(sinusoid(timesteps, model_width)).astype(jnp.bfloat16)
    mod_local = matmul(silu_low, mod_weight) + mod_bias.astype(jnp.float32)
    modulation = lax.all_gather(mod_local, "tensor", axis=1, tiled=True)

    def token_mod(component):
        return jnp.dot(
            onehot,
            modulation[:, component * model_width : (component + 1) * model_width],
            precision=lax.Precision.HIGHEST,
            preferred_element_type=jnp.float32,
        )

    shift_one, scale_one, gate_one = (token_mod(0), token_mod(1), token_mod(2))
    shift_two, scale_two, gate_two = (token_mod(3), token_mod(4), token_mod(5))
    shift_three, scale_three, gate_three = (token_mod(6), token_mod(7), token_mod(8))
    layer_in = tokens.astype(jnp.float32)
    normed_one, inverse_one = normalize(layer_in)
    hidden_one = (normed_one * (1.0 + scale_one) + shift_one).astype(jnp.bfloat16)
    queries = matmul(hidden_one, q_weight).astype(jnp.bfloat16)
    key_rows = matmul(hidden_one, k_weight).astype(jnp.bfloat16)
    value_rows = matmul(hidden_one, v_weight).astype(jnp.bfloat16)
    attended, self_sums = attend_forward(queries, key_rows, value_rows, self_allowed, score_scale)
    attended = attended.astype(jnp.bfloat16)
    branch_one = lax.psum(matmul(attended, o_weight).astype(jnp.bfloat16), "tensor").astype(
        jnp.float32
    )
    after_one = layer_in + gate_one * branch_one
    normed_two, inverse_two = normalize(after_one)
    hidden_two = (normed_two * (1.0 + scale_two) + shift_two).astype(jnp.bfloat16)
    cross_queries = matmul(hidden_two, cross_q).astype(jnp.bfloat16)
    text_flat = text_states.reshape(slot_count * text_rows, text_states.shape[2])
    text_keys = matmul(text_flat, cross_k).astype(jnp.bfloat16)
    text_values = matmul(text_flat, cross_v).astype(jnp.bfloat16)
    crossed, cross_sums = attend_forward(
        cross_queries, text_keys, text_values, cross_allowed, score_scale
    )
    crossed = crossed.astype(jnp.bfloat16)
    branch_two = lax.psum(matmul(crossed, cross_o).astype(jnp.bfloat16), "tensor").astype(
        jnp.float32
    )
    after_two = after_one + gate_two * branch_two
    normed_three, inverse_three = normalize(after_two)
    hidden_three = (normed_three * (1.0 + scale_three) + shift_three).astype(jnp.bfloat16)
    pre_act = matmul(hidden_three, mlp_in)
    activated = jax.nn.gelu(pre_act, approximate=True).astype(jnp.bfloat16)
    branch_three = lax.psum(matmul(activated, mlp_out).astype(jnp.bfloat16), "tensor").astype(
        jnp.float32
    )
    output_rows = (after_two + gate_three * branch_three).astype(jnp.bfloat16)
    grad_out = cotangent.astype(jnp.float32)
    gate_three_grad = grad_out * branch_three
    branch_three_grad = (grad_out * gate_three).astype(jnp.bfloat16)
    mlp_out_grad = matmul_tn(activated, branch_three_grad)
    act_grad = matmul_nt(branch_three_grad, mlp_out)
    unused_value, gelu_pull = jax.vjp(lambda v: jax.nn.gelu(v, approximate=True), pre_act)
    pre_grad = gelu_pull(act_grad)[0].astype(jnp.bfloat16)
    mlp_in_grad = matmul_tn(hidden_three, pre_grad)
    hidden_three_grad = lax.psum(matmul_nt(pre_grad, mlp_in).astype(jnp.bfloat16), "tensor").astype(
        jnp.float32
    )
    after_two_grad = grad_out + norm_back(
        hidden_three_grad * (1.0 + scale_three), normed_three, inverse_three
    )
    gate_two_grad = after_two_grad * branch_two
    branch_two_grad = (after_two_grad * gate_two).astype(jnp.bfloat16)
    cross_o_grad = matmul_tn(crossed, branch_two_grad)
    crossed_grad = matmul_nt(branch_two_grad, cross_o).astype(jnp.bfloat16)
    cross_query_grad, text_key_grad, text_value_grad = attend_backward(
        cross_queries, text_keys, text_values, cross_allowed, score_scale, cross_sums, crossed_grad
    )
    cross_query_grad = cross_query_grad.astype(jnp.bfloat16)
    text_key_grad = text_key_grad.astype(jnp.bfloat16)
    text_value_grad = text_value_grad.astype(jnp.bfloat16)
    cross_q_grad = matmul_tn(hidden_two, cross_query_grad)
    cross_k_grad = matmul_tn(text_flat, text_key_grad)
    cross_v_grad = matmul_tn(text_flat, text_value_grad)
    hidden_two_grad = lax.psum(
        matmul_nt(cross_query_grad, cross_q).astype(jnp.bfloat16), "tensor"
    ).astype(jnp.float32)
    after_one_grad = after_two_grad + norm_back(
        hidden_two_grad * (1.0 + scale_two), normed_two, inverse_two
    )
    gate_one_grad = after_one_grad * branch_one
    branch_one_grad = (after_one_grad * gate_one).astype(jnp.bfloat16)
    o_weight_grad = matmul_tn(attended, branch_one_grad)
    attended_grad = matmul_nt(branch_one_grad, o_weight).astype(jnp.bfloat16)
    query_grad, key_grad, value_grad = attend_backward(
        queries, key_rows, value_rows, self_allowed, score_scale, self_sums, attended_grad
    )
    query_grad = query_grad.astype(jnp.bfloat16)
    key_grad = key_grad.astype(jnp.bfloat16)
    value_grad = value_grad.astype(jnp.bfloat16)
    q_weight_grad = matmul_tn(hidden_one, query_grad)
    k_weight_grad = matmul_tn(hidden_one, key_grad)
    v_weight_grad = matmul_tn(hidden_one, value_grad)
    hidden_partial = (
        matmul_nt(query_grad, q_weight)
        + matmul_nt(key_grad, k_weight)
        + matmul_nt(value_grad, v_weight)
    )
    hidden_one_grad = lax.psum(hidden_partial.astype(jnp.bfloat16), "tensor").astype(jnp.float32)
    token_grad = (
        after_one_grad + norm_back(hidden_one_grad * (1.0 + scale_one), normed_one, inverse_one)
    ).astype(jnp.bfloat16)
    token_terms = [
        hidden_one_grad,
        hidden_one_grad * normed_one,
        gate_one_grad,
        hidden_two_grad,
        hidden_two_grad * normed_two,
        gate_two_grad,
        hidden_three_grad,
        hidden_three_grad * normed_three,
        gate_three_grad,
    ]
    slot_grad = jnp.concatenate([exact_tn(onehot, term) for term in token_terms], axis=1).astype(
        jnp.bfloat16
    )
    local_cols = mod_weight.shape[1]
    local_grad = lax.dynamic_slice_in_dim(
        slot_grad, lax.axis_index("tensor") * local_cols, local_cols, 1
    )
    mod_weight_grad = matmul_tn(silu_low, local_grad)
    mod_bias_grad = jnp.sum(local_grad.astype(jnp.float32), axis=0)
    (
        q_weight_grad,
        k_weight_grad,
        v_weight_grad,
        o_weight_grad,
        cross_q_grad,
        cross_k_grad,
        cross_v_grad,
        cross_o_grad,
        mlp_in_grad,
        mlp_out_grad,
        mod_weight_grad,
        mod_bias_grad,
    ) = (
        lax.psum(q_weight_grad.astype(jnp.bfloat16), "dp").astype(jnp.float32),
        lax.psum(k_weight_grad.astype(jnp.bfloat16), "dp").astype(jnp.float32),
        lax.psum(v_weight_grad.astype(jnp.bfloat16), "dp").astype(jnp.float32),
        lax.psum(o_weight_grad.astype(jnp.bfloat16), "dp").astype(jnp.float32),
        lax.psum(cross_q_grad.astype(jnp.bfloat16), "dp").astype(jnp.float32),
        lax.psum(cross_k_grad.astype(jnp.bfloat16), "dp").astype(jnp.float32),
        lax.psum(cross_v_grad.astype(jnp.bfloat16), "dp").astype(jnp.float32),
        lax.psum(cross_o_grad.astype(jnp.bfloat16), "dp").astype(jnp.float32),
        lax.psum(mlp_in_grad.astype(jnp.bfloat16), "dp").astype(jnp.float32),
        lax.psum(mlp_out_grad.astype(jnp.bfloat16), "dp").astype(jnp.float32),
        lax.psum(mod_weight_grad.astype(jnp.bfloat16), "dp").astype(jnp.float32),
        lax.psum(mod_bias_grad.astype(jnp.bfloat16), "dp").astype(jnp.float32),
    )
    return (
        output_rows,
        token_grad,
        q_weight_grad,
        k_weight_grad,
        v_weight_grad,
        o_weight_grad,
        cross_q_grad,
        cross_k_grad,
        cross_v_grad,
        cross_o_grad,
        mlp_in_grad,
        mlp_out_grad,
        mod_weight_grad,
        mod_bias_grad,
    )


def solution(mesh):
    placed = (
        P("dp", None),
        P("dp", None, None),
        P("dp"),
        P("dp"),
        P("dp"),
        P(None, "tensor"),
        P(None, "tensor"),
        P(None, "tensor"),
        P("tensor", None),
        P(None, "tensor"),
        P(None, "tensor"),
        P(None, "tensor"),
        P("tensor", None),
        P(None, "tensor"),
        P("tensor", None),
        P(None, "tensor"),
        P("tensor"),
        P("dp", None),
    )
    return jax.shard_map(
        local,
        mesh=mesh,
        in_specs=placed,
        out_specs=(
            P("dp", None),
            P("dp", None),
            P(None, "tensor"),
            P(None, "tensor"),
            P(None, "tensor"),
            P("tensor", None),
            P(None, "tensor"),
            P(None, "tensor"),
            P(None, "tensor"),
            P("tensor", None),
            P(None, "tensor"),
            P("tensor", None),
            P(None, "tensor"),
            P("tensor"),
        ),
        check_vma=False,
    )
```

profile of v0, /device:TPU:0, one launch (start us, length us, event | category | flops | bytes accessed | tf_op | source)
XLA Modules:
  0.0 669.6 jit_solution(3544904661977503280)
XLA Ops:
  10.6 6.5 all-gather
  44.2 3.9 fusion.104
  48.0 3.9 fusion.106
  52.0 32.7 %all-reduce.9.cloned.1.call-done = bf16[1024,768]{0,1:T(8,128)(2,1)} async-done(((bf16[1024,768]{0,1:T(8,128)(2,1)}), bf16[1024,768]{0,1:T(8,128)(2,1)}) %all-reduce.9.cloned.1.call-update) | async-done | bytes 1572880 | tf_op jit(solution)/shard_map/psum | solution.py:209
  84.7 5.4 fusion.166
  105.1 3.9 fusion.105
  110.2 35.5 %all-reduce.11.cloned.1.call-done = bf16[1024,768]{0,1:T(8,128)(2,1)} async-done(((bf16[1024,768]{0,1:T(8,128)(2,1)}), bf16[1024,768]{0,1:T(8,128)(2,1)}) %all-reduce.11.cloned.1.call-update) | async-done | bytes 1572880 | tf_op jit(solution)/shard_map/psum | solution.py:223
  145.7 5.8 fusion.164
  153.4 2.9 add_convert_fusion.1
  163.1 3.3 fusion.31
  170.4 4.5 convolution_convert_fusion.7
  174.9 3.1 convolution_convert_fusion.6
  178.0 35.1 %all-reduce.13.cloned.1.call-done = bf16[1024,768]{0,1:T(8,128)(2,1)} async-done(((bf16[1024,768]{0,1:T(8,128)(2,1)}), bf16[1024,768]{0,1:T(8,128)(2,1)}) %all-reduce.13.cloned.1.call-update) | async-done | bytes 1572880 | tf_op jit(solution)/shard_map/psum | solution.py:243
  213.2 3.5 fusion.92
  217.4 5.2 multiply_convert_fusion.3
  240.4 34.7 %all-reduce.15.cloned.1.call-done = bf16[1024,768]{0,1:T(8,128)(2,1)} async-done(((bf16[1024,768]{0,1:T(8,128)(2,1)}), bf16[1024,768]{0,1:T(8,128)(2,1)}) %all-reduce.15.cloned.1.call-update) | async-done | bytes 1572880 | tf_op jit(solution)/shard_map/psum | solution.py:262
  275.2 4.3 fusion.93
  280.7 6.5 multiply_convert_fusion.2
  317.7 56.7 %all-reduce.19.cloned.1.call-done = (bf16[1024,768]{0,1:T(8,128)(2,1)}, bf16[1024,768]{0,1:T(8,128)(2,1)}) async-done(((bf16[1024,768]{0,1:T(8,128)(2,1)}, bf16[1024,768]{0,1:T(8,128)(2,1)}), (bf16[1024,768]{0,1:T(8,128)(2,1)}, bf16[1024,768]{0,1:T(8,128)(2,1)})) %all-reduce.19.cloned.1.call-update) | async-done | bytes 3145744 | tf_op jit(solution)/shard_map/psum | solution.py:231
  376.8 4.1 fusion.86
  395.8 4.4 fusion.21
  403.8 3.0 fusion.94
  412.8 22.4 %psum.143 = bf16[1728]{0:T(1024)(128)(2,1)S(1)} all-reduce(bf16[1728]{0:T(1024)(128)(2,1)S(1)} %dynamic-slice_reduce_fusion), channel_id=1, replica_groups=mesh['dp'=8,'tensor'=4] {'dp'}, use_global_device_ids=true, to_apply=%region_44.45 | all-reduce | flops 1728 | bytes 6912 | tf_op jit(solution)/shard_map/psum | solution.py:335
  435.8 209.9 %all-reduce.17.cloned.1.call-done = (bf16[768,192]{0,1:T(8,128)(2,1)}, bf16[768,192]{0,1:T(8,128)(2,1)}, bf16[768,192]{0,1:T(8,128)(2,1)}, bf16[192,768]{1,0:T(8...) async-done(((bf16[768,192]{0,1:T(8,128)(2,1)}, ...) | async-done | bytes 7372816 | tf_op jit(solution)/shard_map/psum | solution.py:324
  (405 shorter events, 152.2 us)
Async XLA Ops:
  7.2 77.5 %all-reduce.9.cloned.1.call-start = ((), (), s32[]{:S(2)}) async-start(), calls=%async_computation | async-start | bytes 3145728 | tf_op jit(solution)/shard_map/psum | solution.py:209
  9.8 9.2 %copy-start.115 = (f32[4,384]{1,0:T(4,128)}, f32[4,384]{1,0:T(4,128)S(1)}, u32[]{:S(2)}) copy-start(f32[4,384]{1,0:T(4,128)S(1)} %get-tuple-element.109) | copy-start | bytes 18436
  9.8 9.2 %copy-start.117 = (f32[4,384]{1,0:T(4,128)}, f32[4,384]{1,0:T(4,128)S(1)}, u32[]{:S(2)}) copy-start(f32[4,384]{1,0:T(4,128)S(1)} %get-tuple-element.110) | copy-start | bytes 18436
  10.6 8.4 %copy-start.61 = (bf16[1024,768]{1,0:T(8,128)(2,1)S(1)}, bf16[1024,768]{1,0:T(8,128)(2,1)}, u32[]{:S(2)}) copy-start(bf16[1024,768]{1,0:T(8,128)(2,1)} %param.18) | copy-start | bytes 4718596
  24.9 10.1 %copy-start.48 = (bf16[1024,192]{0,1:T(8,128)(2,1)}, bf16[1024,192]{0,1:T(8,128)(2,1)S(1)}, u32[]{:S(2)}) copy-start(bf16[1024,192]{0,1:T(8,128)(2,1)S(1)} %convolution_convert_fusion.13) | copy-start | bytes 1179652
  40.0 105.7 %all-reduce.11.cloned.1.call-start = ((), (), s32[]{:S(2)}) async-start(), calls=%async_computation.1 | async-start | bytes 3145728 | tf_op jit(solution)/shard_map/psum | solution.py:223
  41.5 10.5 %copy-start.35 = (bf16[308,768]{1,0:T(8,128)(2,1)}, bf16[308,768]{1,0:T(8,128)(2,1)S(1)}, u32[]{:S(2)}) copy-start(bf16[308,768]{1,0:T(8,128)(2,1)S(1)} %reshape.268) | copy-start | bytes 1419268
  102.6 110.5 %all-reduce.13.cloned.1.call-start = ((), (), s32[]{:S(2)}) async-start(), calls=%async_computation.2 | async-start | bytes 3145728 | tf_op jit(solution)/shard_map/psum | solution.py:243
  170.1 105.0 %all-reduce.15.cloned.1.call-start = ((), (), s32[]{:S(2)}) async-start(), calls=%async_computation.3 | async-start | bytes 3145728 | tf_op jit(solution)/shard_map/psum | solution.py:262
  232.1 142.4 %all-reduce.19.cloned.1.call-start = ((), (), s32[]{:S(2)}) async-start(), calls=%async_computation.5 | async-start | bytes 6291456 | tf_op jit(solution)/shard_map/psum | solution.py:231
  279.5 9.6 %slice-start = ((s8[6291456]{0:T(1024)(128)(4,1)}), s8[4194304]{0:T(1024)(128)(4,1)S(1)}, s32[]{:S(2)}) async-start(s8[6291456]{0:T(1024)(128)(4,1)} %bitcast.149), calls=%async_computation.6 | async-start | bytes 8388608
  280.7 8.3 %slice-start.1 = ((s8[6291456]{0:T(1024)(128)(4,1)}), s8[2097152]{0:T(1024)(128)(4,1)S(1)}, s32[]{:S(2)}) async-start(s8[6291456]{0:T(1024)(128)(4,1)} %bitcast.149), calls=%async_computation.7 | async-start | bytes 4194304
  280.7 8.3 %copy-start.101 = (f32[3,512]{1,0:T(4,128)S(1)}, f32[3,512]{1,0:T(4,128)}, u32[]{:S(2)}) copy-start(f32[3,512]{1,0:T(4,128)} %log_add_fusion.1) | copy-start | bytes 18436
  293.9 9.2 %copy-start.81 = (bf16[3,64,512]{2,1,0:T(8,128)(2,1)}, bf16[3,64,512]{2,1,0:T(8,128)(2,1)S(1)}, u32[]{:S(2)}) copy-start(bf16[3,64,512]{2,1,0:T(8,128)(2,1)S(1)} %fusion.61) | copy-start | bytes 589828
  305.6 340.1 %all-reduce.17.cloned.1.call-start = ((), (), s32[]{:S(2)}) async-start(), calls=%async_computation.4 | async-start | bytes 14745600 | tf_op jit(solution)/shard_map/psum | solution.py:324
  305.8 7.7 %copy-start.23 = (bf16[1024,768]{0,1:T(8,128)(2,1)S(1)}, bf16[1024,768]{0,1:T(8,128)(2,1)}, u32[]{:S(2)}) copy-start(bf16[1024,768]{0,1:T(8,128)(2,1)} %copy-done.22) | copy-start | bytes 4718596
  305.8 7.7 %copy-start.82 = (bf16[3,64,512]{2,1,0:T(8,128)(2,1)S(1)}, bf16[3,64,512]{2,1,0:T(8,128)(2,1)}, u32[]{:S(2)}) copy-start(bf16[3,64,512]{2,1,0:T(8,128)(2,1)} %copy-done.81) | copy-start | bytes 589828
  305.8 7.7 %copy-start.84 = (bf16[3,64,512]{2,1,0:T(8,128)(2,1)S(1)}, bf16[3,64,512]{2,1,0:T(8,128)(2,1)}, u32[]{:S(2)}) copy-start(bf16[3,64,512]{2,1,0:T(8,128)(2,1)} %copy-done.83) | copy-start | bytes 589828
  395.8 7.2 %copy-start.114 = (f32[1024]{0:T(1024)S(1)}, f32[1024]{0:T(1024)}, u32[]{:S(2)}) copy-start(f32[1024]{0:T(1024)} %copy-done.113) | copy-start | bytes 12292
  645.7 7.5 %copy-start.94 = (bf16[768,192]{0,1:T(8,128)(2,1)S(1)}, bf16[768,192]{0,1:T(8,128)(2,1)}, u32[]{:S(2)}) copy-start(bf16[768,192]{0,1:T(8,128)(2,1)} %get-tuple-element.80) | copy-start | bytes 884740
  645.7 8.3 %copy-start.93 = (bf16[768,192]{0,1:T(8,128)(2,1)S(1)}, bf16[768,192]{0,1:T(8,128)(2,1)}, u32[]{:S(2)}) copy-start(bf16[768,192]{0,1:T(8,128)(2,1)} %get-tuple-element.81) | copy-start | bytes 884740
  645.7 9.2 %copy-start.92 = (bf16[768,192]{0,1:T(8,128)(2,1)S(1)}, bf16[768,192]{0,1:T(8,128)(2,1)}, u32[]{:S(2)}) copy-start(bf16[768,192]{0,1:T(8,128)(2,1)} %get-tuple-element.82) | copy-start | bytes 884740
  645.7 10.0 %copy-start.91 = (bf16[192,768]{1,0:T(8,128)(2,1)S(1)}, bf16[192,768]{1,0:T(8,128)(2,1)}, u32[]{:S(2)}) copy-start(bf16[192,768]{1,0:T(8,128)(2,1)} %get-tuple-element.83) | copy-start | bytes 884740
  647.6 9.0 %copy-start.74 = (bf16[768,768]{1,0:T(8,128)(2,1)S(1)}, bf16[768,768]{1,0:T(8,128)(2,1)}, u32[]{:S(2)}) copy-start(bf16[768,768]{1,0:T(8,128)(2,1)} %get-tuple-element.84) | copy-start | bytes 3538948
  (113 other events, 339.4 us)
Sparse Core Ops, SparseCore 0:
  40.1 44.5 all-reduce.8
  102.7 42.9 all-reduce.10
  170.2 42.8 all-reduce.12
  232.2 42.9 all-reduce.14
  305.7 68.7 all-reduce.18
  395.9 249.7 all-reduce.16
where the time goes:
time: 680 us; the launch traced here: 670 us
  waiting for transfers between devices  405 us (60%)
  matrix products  128 us (19%)
  other arithmetic  62 us (9%)
  local copies, waits for them, and re-layouts  29.1 us (4%)
  blocking collectives  28.9 us (4%)
  between operations  15.9 us (2%)
    psum x1, waiting for transfers between devices, local(): lax.psum(q_weight_grad.astype(jnp.bfloat16), 'dp').astype(jnp.float32)  210 us
    psum x1, waiting for transfers between devices, local(): lax.psum(matmul(activated, mlp_out).astype(jnp.bfloat16), 'tensor')  56.7 us
    psum x1, waiting for transfers between devices, local(): lax.psum(matmul(crossed, cross_o).astype(jnp.bfloat16), 'tensor')  35.5 us
    psum x1, waiting for transfers between devices, local(): lax.psum(matmul_nt(pre_grad, mlp_in).astype(jnp.bfloat16), 'tensor')  35.1 us
    psum x1, waiting for transfers between devices, local(): lax.psum(matmul_nt(cross_query_grad, cross_q).astype(jnp.bfloat16), 'tens...  34.7 us
    psum x1, waiting for transfers between devices, local(): lax.psum(matmul(attended, o_weight).astype(jnp.bfloat16), 'tensor')  32.7 us
    dot_general x9, matrix products, token_mod(): jnp.dot(onehot, modulation[:, component * model_width:(component + 1) * m...  32.3 us
    unnamed x268, local copies, waits for them, and re-layouts  26.9 us
  transfers between devices with their start and end apart: 6, of which 6 were waited for; matrix products, arithmetic and copies ran while one was open for 9% of the time, Pallas kernels for 0%

commit v1 on v0

v1 whole, which is shorter than its diff:
```python
import math

import jax
import jax.numpy as jnp
from jax import lax
from jax.experimental import pallas as pl
from jax.experimental.pallas import tpu as pltpu
from jax.sharding import PartitionSpec as P

HEAD = 64
BLOCK = 256
EPSILON = 1e-06
MASKED = -1000000000.0
CURVE = math.sqrt(2.0 / math.pi)
CUBIC = 0.044715
F32 = jnp.float32
BF16 = jnp.bfloat16


def dot_nn(a, b):
    return lax.dot_general(a, b, (((1,), (0,)), ((), ())), preferred_element_type=F32)


def dot_nt(a, b):
    return lax.dot_general(a, b, (((1,), (1,)), ((), ())), preferred_element_type=F32)


def dot_tn(a, b):
    return lax.dot_general(a, b, (((0,), (0,)), ((), ())), preferred_element_type=F32)


def normalize(values):
    centered = values - jnp.mean(values, axis=-1, keepdims=True)
    inverse = lax.rsqrt(jnp.mean(centered * centered, axis=-1, keepdims=True) + EPSILON)
    return centered * inverse, inverse


def norm_back(grad, normed, inverse):
    first = jnp.mean(grad, axis=-1, keepdims=True)
    second = jnp.mean(grad * normed, axis=-1, keepdims=True)
    return inverse * (grad - first - normed * second)


def column_sum(values):
    return jnp.sum(values, axis=0, keepdims=True)


def three_parts(column):
    high = column.astype(BF16).astype(F32)
    rest = column - high
    middle = rest.astype(BF16).astype(F32)
    return high, middle, rest - middle


def head_slice(rows, head):
    piece = rows[:, head * HEAD : (head + 1) * HEAD]
    return jnp.concatenate([piece, jnp.zeros_like(piece)], axis=1)


def run(kernel, outs, scalars, arrays, scratch=(), flops=0, vmem=40):
    vmem_spec = pl.BlockSpec(memory_space=pltpu.VMEM)
    return pl.pallas_call(
        kernel,
        out_shape=[jax.ShapeDtypeStruct(shape, kind) for shape, kind in outs],
        in_specs=[pl.BlockSpec(memory_space=pltpu.SMEM)] + [vmem_spec] * len(arrays),
        out_specs=[vmem_spec] * len(outs),
        scratch_shapes=[pltpu.VMEM(shape, kind) for shape, kind in scratch],
        compiler_params=pltpu.CompilerParams(vmem_limit_bytes=vmem * 1024 * 1024),
        cost_estimate=pl.CostEstimate(flops=flops, bytes_accessed=8_000_000, transcendentals=0),
    )(scalars, *arrays)


SLOT, CORE, OWN, ROW, LIMIT = 0, 4, 5, 7, 8


def text_kernel(place, text, ck, cv, cq, co, packed):
    width = ck.shape[1]
    slots = text.shape[0]
    rows = text.shape[1]
    packed[0:width, :] = cq[...].astype(F32).T.astype(BF16)
    packed[width : 2 * width, :] = co[...]
    for slot in range(slots):
        keys = dot_nn(text[slot], ck[...]).astype(BF16)
        values = dot_nn(text[slot], cv[...]).astype(BF16)
        first = 2 * width + rows * (slot % 2)
        left = 2 * width * (slot // 2)
        packed[first : first + rows, left : left + 2 * width] = jnp.concatenate([keys, values], axis=1)


def self_forward(place, tokens, mod, wq, wk, wv, wo, part, h1, qa, ka, va, att):
    model = tokens.shape[1]
    blocks = tokens.shape[0] // BLOCK
    half = blocks // 2
    heads = wq.shape[1] // HEAD
    lane = lax.broadcasted_iota(jnp.int32, (BLOCK, 2 * HEAD), 1)
    keep = lane < HEAD

    def project(block, carry):
        rows = pl.ds(pl.multiple_of(block * BLOCK, BLOCK), BLOCK)
        slot = place[SLOT + block]
        normed, _ = normalize(tokens[rows, :].astype(F32))
        scale = mod[pl.ds(slot, 1), model : 2 * model]
        shift = mod[pl.ds(slot, 1), 0:model]
        hidden = (normed * (1.0 + scale) + shift).astype(BF16)
        h1[rows, :] = hidden
        q = dot_nn(hidden, wq[...]).astype(BF16).astype(F32) * (HEAD**-0.5)
        k = dot_nn(hidden, wk[...])
        v = dot_nn(hidden, wv[...])
        mine = lane == HEAD + slot
        q_more = jnp.where(mine, 1.0, 0.0)
        k_more = jnp.where((lane >= HEAD + 4) & (lane < HEAD + 7), 1.0, 0.0)
        k_more = jnp.where((lane >= HEAD) & (lane < HEAD + 4) & jnp.logical_not(mine), MASKED, k_more)
        v_more = jnp.where((lane >= HEAD) & (lane < HEAD + 3), 1.0, 0.0)
        for head in range(heads):
            qa[head, rows, :] = jnp.where(keep, head_slice(q, head), q_more).astype(BF16)
            ka[head, rows, :] = jnp.where(keep, head_slice(k, head), k_more).astype(BF16)
            va[head, rows, :] = jnp.where(keep, head_slice(v, head), v_more).astype(BF16)
        return carry

    lax.fori_loop(0, blocks, project, 0)

    def attend(block, carry):
        rows = pl.ds(pl.multiple_of(block * BLOCK, BLOCK), BLOCK)
        pieces = []
        for head in range(heads):
            queries = qa[head, rows, :]
            scores = dot_nt(queries, ka[head])
            top = jnp.max(scores, axis=1, keepdims=True)
            raised = jnp.exp(scores - top).astype(BF16)
            out = dot_nn(raised, va[head])
            total = out[:, HEAD : HEAD + 1]
            pieces.append(out[:, :HEAD] * (1.0 / total))
            high, middle, low = three_parts(-(top + jnp.log(total)))
            more = jnp.where(lane == HEAD + 4, high, jnp.where(lane == HEAD + 5, middle, low))
            spot = (lane >= HEAD + 4) & (lane < HEAD + 7)
            qa[head, rows, :] = jnp.where(spot, more, queries.astype(F32)).astype(BF16)
        attended = jnp.concatenate(pieces, axis=1).astype(BF16)
        att[rows, :] = attended
        side = lax.div(block, half) ^ place[CORE]
        out_rows = pl.ds(pl.multiple_of(lax.rem(block, half) * BLOCK, BLOCK), BLOCK)
        part[side, out_rows, :] = dot_nn(attended, wo[...]).astype(BF16)
        return carry

    lax.fori_loop(0, blocks, attend, 0)


def gather_pieces(pieces, cqt, co, width):
    for index, piece in enumerate(pieces):
        cqt[index * width : (index + 1) * width, :] = piece[0:width, :]
        co[index * width : (index + 1) * width, :] = piece[width : 2 * width, :]


def middle_kernel(
    place, tokens, cot, mod, sum_own, sum_far, p0, p1, p2, p3, win0, win1, wout0, wout1,
    x1_out, b2_out, h2_out, q2_out, cr_out, kall, vall, h3g_out, b3_out, dw_out,
    cqt, co, h3_all, act0, act1, pg0, pg1, b3g_all,
):
    model = tokens.shape[1]
    width = (p0.shape[1]) // 4
    rows_of_slot = kall.shape[1]
    count = sum_own.shape[0]
    blocks = count // BLOCK
    pieces = (p0, p1, p2, p3)
    gather_pieces(pieces, cqt, co, width)
    for slot in range(kall.shape[0]):
        first = 2 * width + rows_of_slot * (slot % 2)
        left = 2 * width * (slot // 2)
        both = [p[first : first + rows_of_slot, left : left + 2 * width] for p in pieces]
        kall[slot] = jnp.concatenate([b[:, :width] for b in both], axis=1)
        vall[slot] = jnp.concatenate([b[:, width:] for b in both], axis=1)
    lane = lax.broadcasted_iota(jnp.int32, (1, 2 * HEAD), 1)
    sides = [jnp.where(lane < HEAD, 1.0, 0.0).astype(BF16), jnp.where(lane < HEAD, 0.0, 1.0).astype(BF16)]
    key_lane = lax.broadcasted_iota(jnp.int32, (BLOCK, rows_of_slot), 1)

    def body(block, carry):
        first = pl.multiple_of(block * BLOCK, BLOCK)
        rows = pl.ds(first, BLOCK)
        group_rows = pl.ds(pl.multiple_of(place[CORE] * count + first, BLOCK), BLOCK)
        slot = place[OWN + block]

        def m(component):
            return mod[pl.ds(slot, 1), component * model : (component + 1) * model]

        branch = sum_own[rows, :].astype(F32) + sum_far[rows, :].astype(F32)
        x1 = tokens[group_rows, :].astype(F32) + m(2) * branch
        x1_out[rows, :] = x1
        normed, _ = normalize(x1)
        h2 = (normed * (1.0 + m(4)) + m(3)).astype(BF16)
        h2_out[rows, :] = h2
        q2 = dot_nt(h2, cqt[...]).astype(BF16)
        q2_out[rows, :] = q2
        allowed = key_lane < place[LIMIT + slot]
        crossed = []
        for pair in range(model // (2 * HEAD)):
            cols = slice(pair * 2 * HEAD, (pair + 1) * 2 * HEAD)
            keys = kall[slot, :, cols]
            values = vall[slot, :, cols]
            total = None
            for side in sides:
                scores = dot_nt(q2[:, cols], keys * side) * (HEAD**-0.5)
                scores = jnp.where(allowed, scores, MASKED)
                raised = jnp.exp(scores - jnp.max(scores, axis=1, keepdims=True))
                probs = raised * (1.0 / jnp.sum(raised, axis=1, keepdims=True))
                out = dot_nn(probs.astype(BF16), values * side)
                total = out if total is None else total + out
            crossed.append(total.astype(BF16))
        crossed = jnp.concatenate(crossed, axis=1)
        cr_out[rows, :] = crossed
        b2 = dot_nn(crossed, co[...])
        b2_out[rows, :] = b2
        x2 = x1 + m(5) * b2
        normed, _ = normalize(x2)
        h3 = (normed * (1.0 + m(7)) + m(6)).astype(BF16)
        h3_all[rows, :] = h3
        b3g = (cot[group_rows, :].astype(F32) * m(8)).astype(BF16)
        b3g_all[rows, :] = b3g
        b3 = jnp.zeros((BLOCK, model), F32)
        h3g = jnp.zeros((BLOCK, model), F32)
        for win, wout, act_all, pg_all in ((win0, wout0, act0, pg0), (win1, wout1, act1, pg1)):
            pre = dot_nn(h3, win[...])
            square = pre * pre
            bent = jnp.tanh(CURVE * (pre + CUBIC * (square * pre)))
            act = (0.5 * pre * (1.0 + bent)).astype(BF16)
            act_all[rows, :] = act
            slope = 0.5 * (1.0 + bent) + 0.5 * pre * (1.0 - bent * bent) * (
                CURVE * (1.0 + 3.0 * CUBIC * square)
            )
            b3 = b3 + dot_nn(act, wout[...])
            pg = (dot_nt(b3g, wout[...]) * slope).astype(BF16)
            pg_all[rows, :] = pg
            h3g = h3g + dot_nt(pg, win[...])
        b3_out[rows, :] = b3.astype(BF16)
        h3g_out[rows, :] = h3g.astype(BF16)
        return carry

    lax.fori_loop(0, blocks, body, 0)
    row = place[ROW]
    for member, (act_all, pg_all) in enumerate(((act0, pg0), (act1, pg1))):
        for start in range(0, model, BLOCK):
            cols = slice(start, start + BLOCK)
            dw_out[member, row, cols, :] = dot_tn(h3_all[:, cols], pg_all[...]).astype(BF16)
            dw_out[member, 1 - row, cols, :] = dot_tn(act_all[:, cols], b3g_all[...]).astype(BF16)


def cross_back(
    place, mod, cot, text, h3g_own, h3g_far, x1_in, b2_in, sum_own, sum_far, h2_in, q2_in, cr_in,
    kall, vall, p0, p1, p2, p3,
    b1g_out, x1g_out, dw_out, sums,
    cqt, co, dk_all, dv_all, dq_all, b2g_all,
):
    model = cot.shape[1]
    width = p0.shape[1] // 4
    rows_of_slot = kall.shape[1]
    count = sum_own.shape[0]
    blocks = count // BLOCK
    gather_pieces((p0, p1, p2, p3), cqt, co, width)
    dk_all[...] = jnp.zeros_like(dk_all)
    dv_all[...] = jnp.zeros_like(dv_all)
    lane = lax.broadcasted_iota(jnp.int32, (1, 2 * HEAD), 1)
    sides = [jnp.where(lane < HEAD, 1.0, 0.0), jnp.where(lane < HEAD, 0.0, 1.0)]
    key_row = lax.broadcasted_iota(jnp.int32, (rows_of_slot, BLOCK), 0)

    def body(block, carry):
        first = pl.multiple_of(block * BLOCK, BLOCK)
        rows = pl.ds(first, BLOCK)
        group_rows = pl.ds(pl.multiple_of(place[CORE] * count + first, BLOCK), BLOCK)
        slot = place[OWN + block]

        def m(component):
            return mod[pl.ds(slot, 1), component * model : (component + 1) * model]

        x1 = x1_in[rows, :]
        b2 = b2_in[rows, :]
        h3g = h3g_own[rows, :].astype(F32) + h3g_far[rows, :].astype(F32)
        normed, inverse = normalize(x1 + m(5) * b2)
        sums[block, 4:5, :] = column_sum(h3g)
        sums[block, 5:6, :] = column_sum(h3g * normed)
        x2g = cot[group_rows, :].astype(F32) + norm_back(h3g * (1.0 + m(7)), normed, inverse)
        sums[block, 3:4, :] = column_sum(x2g * b2)
        b2g = (x2g * m(5)).astype(BF16)
        b2g_all[rows, :] = b2g
        out_grad = dot_nt(b2g, co[...]).astype(BF16)
        q2 = q2_in[rows, :]
        allowed = key_row < place[LIMIT + slot]
        query_grads = []
        for pair in range(model // (2 * HEAD)):
            cols = slice(pair * 2 * HEAD, (pair + 1) * 2 * HEAD)
            keys = kall[slot, :, cols]
            values = vall[slot, :, cols]
            queries = q2[:, cols]
            grads = out_grad[:, cols]
            dq = dk = dv = None
            for side in sides:
                side_low = side.astype(BF16)
                key_side = keys * side_low
                scores = jnp.where(allowed, dot_nt(key_side, queries) * (HEAD**-0.5), MASKED)
                raised = jnp.exp(scores - jnp.max(scores, axis=0, keepdims=True))
                probs = raised * (1.0 / jnp.sum(raised, axis=0, keepdims=True))
                prob_grad = dot_nt(values * side_low, grads)
                row_dot = jnp.sum(probs * prob_grad, axis=0, keepdims=True)
                score_grad = (probs * (prob_grad - row_dot)).astype(BF16)
                dv_side = dot_nn(probs.astype(BF16), grads) * side
                dk_side = dot_nn(score_grad, queries) * side
                dq_side = dot_tn(score_grad, key_side)
                dv = dv_side if dv is None else dv + dv_side
                dk = dk_side if dk is None else dk + dk_side
                dq = dq_side if dq is None else dq + dq_side
            query_grads.append((dq * (HEAD**-0.5)).astype(BF16))
            dk_all[slot, :, cols] += dk * (HEAD**-0.5)
            dv_all[slot, :, cols] += dv
        query_grad = jnp.concatenate(query_grads, axis=1)
        dq_all[rows, :] = query_grad
        h2g = dot_nn(query_grad, cqt[...])
        normed, inverse = normalize(x1)
        sums[block, 1:2, :] = column_sum(h2g)
        sums[block, 2:3, :] = column_sum(h2g * normed)
        x1g = x2g + norm_back(h2g * (1.0 + m(4)), normed, inverse)
        x1g_out[rows, :] = x1g
        branch = sum_own[rows, :].astype(F32) + sum_far[rows, :].astype(F32)
        sums[block, 0:1, :] = column_sum(x1g * branch)
        b1g_out[rows, :] = (x1g * m(2)).astype(BF16)
        return carry

    lax.fori_loop(0, blocks, body, 0)
    flip = 2 * place[ROW]
    for member in range(2):
        start = (member * width // 128) * 128
        skip = member * width - start
        cols = slice(start, start + 2 * 128)
        kept = slice(skip, skip + width)
        dw_out[member, 0 ^ flip] = dot_tn(dq_all[:, cols], h2_in[...])[kept].astype(BF16)
        dk_rows = dv_rows = None
        for slot in range(kall.shape[0]):
            dk_one = dot_tn(dk_all[slot, :, cols].astype(BF16), text[slot])
            dv_one = dot_tn(dv_all[slot, :, cols].astype(BF16), text[slot])
            dk_rows = dk_one if dk_rows is None else dk_rows + dk_one
            dv_rows = dv_one if dv_rows is None else dv_rows + dv_one
        dw_out[member, 1 ^ flip] = dk_rows[kept].astype(BF16)
        dw_out[member, 2 ^ flip] = dv_rows[kept].astype(BF16)
        dw_out[member, 3 ^ flip] = dot_tn(cr_in[:, cols], b2g_all[...])[kept].astype(BF16)


def self_back(
    place, b1g_own, b1g_far, att, h1, qa, ka, va, wq, wk, wv, wo,
    part, dw_out,
    b1g, da, dq_sum, dq_all, dk_all, dv_all,
):
    count = b1g_own.shape[0]
    blocks = h1.shape[0] // BLOCK
    half = blocks // 2
    heads = wq.shape[1] // HEAD
    b1g[pl.ds(pl.multiple_of(place[CORE] * count, BLOCK), count), :] = b1g_own[...]
    b1g[pl.ds(pl.multiple_of((1 - place[CORE]) * count, BLOCK), count), :] = b1g_far[...]
    dq_sum[...] = jnp.zeros_like(dq_sum)
    lane = lax.broadcasted_iota(jnp.int32, (BLOCK, 2 * HEAD), 1)

    def prepare(block, carry):
        rows = pl.ds(pl.multiple_of(block * BLOCK, BLOCK), BLOCK)
        grads = dot_nt(b1g[rows, :], wo[...]).astype(BF16).astype(F32)
        dots = grads * att[rows, :].astype(F32)
        for head in range(heads):
            row_dot = jnp.sum(dots[:, head * HEAD : (head + 1) * HEAD], axis=1, keepdims=True)
            high, middle, low = three_parts(-row_dot)
            more = jnp.where(lane == HEAD, high, jnp.where(lane == HEAD + 1, middle, low))
            more = jnp.where(lane < HEAD + 3, more, 0.0)
            da[head, rows, :] = jnp.where(lane < HEAD, head_slice(grads, head), more).astype(BF16)
        return carry

    lax.fori_loop(0, blocks, prepare, 0)

    def by_keys(block, carry):
        rows = pl.ds(pl.multiple_of(block * BLOCK, BLOCK), BLOCK)
        dks = []
        dvs = []
        for head in range(heads):
            keys = ka[head, rows, :]
            probs = jnp.exp(dot_nt(keys, qa[head]))
            prob_grad = dot_nt(va[head, rows, :], da[head])
            score_grad = (probs * prob_grad).astype(BF16)
            dvs.append(dot_nn(probs.astype(BF16), da[head])[:, :HEAD])
            dks.append(dot_nn(score_grad, qa[head])[:, :HEAD])
            dq_sum[head] += dot_tn(score_grad, keys)
        dk_all[rows, :] = jnp.concatenate(dks, axis=1).astype(BF16)
        dv_all[rows, :] = jnp.concatenate(dvs, axis=1).astype(BF16)
        return carry

    lax.fori_loop(0, blocks, by_keys, 0)

    def leave(block, carry):
        rows = pl.ds(pl.multiple_of(block * BLOCK, BLOCK), BLOCK)
        dq = jnp.concatenate([dq_sum[head, rows, :HEAD] for head in range(heads)], axis=1)
        dq = (dq * (HEAD**-0.5)).astype(BF16)
        dq_all[rows, :] = dq
        out = dot_nt(dq, wq[...]) + dot_nt(dk_all[rows, :], wk[...]) + dot_nt(dv_all[rows, :], wv[...])
        side = lax.div(block, half) ^ place[CORE]
        out_rows = pl.ds(pl.multiple_of(lax.rem(block, half) * BLOCK, BLOCK), BLOCK)
        part[side, out_rows, :] = out.astype(BF16)
        return carry

    lax.fori_loop(0, blocks, leave, 0)
    flip = 2 * place[ROW]
    dw_out[0 ^ flip] = dot_tn(dq_all[...], h1[...]).astype(BF16)
    dw_out[1 ^ flip] = dot_tn(dk_all[...], h1[...]).astype(BF16)
    dw_out[2 ^ flip] = dot_tn(dv_all[...], h1[...]).astype(BF16)
    dw_out[3 ^ flip] = dot_tn(att[...], b1g[...]).astype(BF16)


def mixed_kernel(place, mod, cot, x1_in, b2_in, b3_own, b3_far, mixed, sums):
    model = cot.shape[1]
    count = x1_in.shape[0]
    for block in range(count // BLOCK):
        rows = slice(block * BLOCK, (block + 1) * BLOCK)
        group_rows = pl.ds(pl.multiple_of(place[CORE] * count + block * BLOCK, BLOCK), BLOCK)
        slot = place[OWN + block]
        gate_two = mod[pl.ds(slot, 1), 5 * model : 6 * model]
        gate_three = mod[pl.ds(slot, 1), 8 * model : 9 * model]
        b3 = b3_own[rows, :].astype(F32) + b3_far[rows, :].astype(F32)
        mixed[rows, :] = (x1_in[rows, :] + gate_two * b2_in[rows, :] + gate_three * b3).astype(BF16)
        sums[block] = column_sum(cot[group_rows, :].astype(F32) * b3)


def final_kernel(place, mod, tokens, h1g_own, h1g_far, x1g_in, sums_cross, sums_mixed, token_grad, slot_sums):
    model = tokens.shape[1]
    count = x1g_in.shape[0]
    slot_sums[...] = jnp.zeros_like(slot_sums)
    for block in range(count // BLOCK):
        rows = slice(block * BLOCK, (block + 1) * BLOCK)
        group_rows = pl.ds(pl.multiple_of(place[CORE] * count + block * BLOCK, BLOCK), BLOCK)
        slot = place[OWN + block]
        h1g = h1g_own[rows, :].astype(F32) + h1g_far[rows, :].astype(F32)
        normed, inverse = normalize(tokens[group_rows, :].astype(F32))
        scale = mod[pl.ds(slot, 1), model : 2 * model]
        token_grad[rows, :] = (x1g_in[rows, :] + norm_back(h1g * (1.0 + scale), normed, inverse)).astype(BF16)
        terms = [column_sum(h1g), column_sum(h1g * normed)]
        terms += [sums_cross[block, i : i + 1, :] for i in range(6)]
        terms += [sums_mixed[block]]
        for component, term in enumerate(terms):
            slot_sums[pl.ds(slot, 1), component * model : (component + 1) * model] += term


def solution(mesh):
    n_dp = mesh.shape["dp"]
    n_tensor = mesh.shape["tensor"]
    core_pairs = [(i, i ^ 1) for i in range(n_tensor)]
    far_pairs = [(i, i ^ 2) for i in range(n_tensor)]
    cross_pairs = [(i, i ^ 3) for i in range(n_tensor)]
    dp_bits = int(math.log2(n_dp))

    def core_swap(value):
        return lax.ppermute(value, "tensor", core_pairs)

    def far_swap(value):
        return lax.ppermute(value, "tensor", far_pairs)

    def dp_swap(value, bit):
        return lax.ppermute(value, "dp", [(i, i ^ (1 << bit)) for i in range(n_dp)])

    def pair_up(flag, mine, other):
        return jnp.concatenate([jnp.where(flag == 0, mine, other), jnp.where(flag == 0, other, mine)], axis=0)

    def local(
        tokens, text_states, clip_len, text_len, timesteps, q_weight, k_weight, v_weight, o_weight,
        cross_q, cross_k, cross_v, cross_o, mlp_in, mlp_out, mod_weight, mod_bias, cotangent,
    ):
        count, model = tokens.shape
        slots, text_rows = text_states.shape[:2]
        width = q_weight.shape[1]
        heads = width // HEAD
        half = count // 2
        blocks = count // BLOCK
        text_pad = -(-text_rows // 16) * 16
        tensor_at = lax.axis_index("tensor")
        dp_at = lax.axis_index("dp")
        core = tensor_at & 1
        row = dp_at & 1

        ends = jnp.cumsum(clip_len)
        starts = jnp.arange(blocks, dtype=jnp.int32) * BLOCK
        slot_of = jnp.sum((starts[:, None] >= ends[None, :]).astype(jnp.int32), axis=1)
        own_slots = lax.dynamic_slice(slot_of, (core * (blocks // 2),), (blocks // 2,))
        place = jnp.concatenate([slot_of, core[None], own_slots, row[None], text_len]).astype(jnp.int32)

        half_width = model // 2
        ramp = jnp.arange(half_width).astype(F32)
        frequency = jnp.exp(ramp * (-math.log(10000.0) / half_width))
        angles = timesteps.astype(F32)[:, None] * frequency[None, :]
        embed = jnp.concatenate([jnp.cos(angles), jnp.sin(angles)], axis=1)
        silu_low = jax.nn.silu(embed).astype(BF16)
        mod_own = dot_nn(silu_low, mod_weight) + mod_bias.astype(F32)
        mod_all = jnp.stack(
            [mod_own] + [lax.ppermute(mod_own, "tensor", p) for p in (core_pairs, far_pairs, cross_pairs)]
        )
        mod = jnp.concatenate(
            [lax.dynamic_index_in_dim(mod_all, tensor_at ^ j, 0, keepdims=False) for j in range(n_tensor)], axis=1
        )

        text = jnp.pad(text_states, ((0, 0), (0, text_pad - text_rows), (0, 0)))
        packed_rows = 2 * width + 2 * text_pad
        (p0,) = run(
            text_kernel, [((packed_rows, model), BF16)], place,
            [text, cross_k, cross_v, cross_q, cross_o], flops=2 * slots * text_pad * model * 2 * width,
        )
        p2 = far_swap(p0)
        p1 = core_swap(p0)
        p3 = core_swap(p2)
        mlp_in_far = core_swap(mlp_in)
        mlp_out_far = core_swap(mlp_out)

        part, h1, qa, ka, va, att = run(
            self_forward,
            [((2, half, model), BF16), ((count, model), BF16)]
            + [((heads, count, 2 * HEAD), BF16)] * 3 + [((count, width), BF16)],
            place, [tokens, mod, q_weight, k_weight, v_weight, o_weight],
            flops=12_000_000_000,
        )
        sum_own = (part[0].astype(F32) + core_swap(part[1]).astype(F32)).astype(BF16)
        sum_far = far_swap(sum_own)

        x1, b2, h2, q2, crossed, kall, vall, h3g_own, b3_own, dw_mlp = run(
            middle_kernel,
            [((half, model), F32)] * 2 + [((half, model), BF16)] * 3
            + [((slots, text_pad, model), BF16)] * 2 + [((half, model), BF16)] * 2
            + [((2, 2, model, model), BF16)],
            place,
            [tokens, cotangent, mod, sum_own, sum_far, p0, p1, p2, p3, mlp_in, mlp_in_far, mlp_out, mlp_out_far],
            scratch=[((model, model), BF16)] * 2 + [((half, model), BF16)] * 6,
            flops=16_000_000_000, vmem=52,
        )
        h3g_far = far_swap(h3g_own)
        dw_mlp = (dw_mlp[0].astype(F32) + core_swap(dw_mlp[1]).astype(F32)).astype(BF16)

        b1g, x1g, dw_cross, sums_cross = run(
            cross_back,
            [((half, model), BF16), ((half, model), F32), ((2, 4, width, model), BF16), ((2, 8, model), F32)],
            place,
            [mod, cotangent, text, h3g_own, h3g_far, x1, b2, sum_own, sum_far, h2, q2, crossed, kall, vall,
             p0, p1, p2, p3],
            scratch=[((model, model), BF16)] * 2 + [((slots, text_pad, model), F32)] * 2 + [((half, model), BF16)] * 2,
            flops=8_000_000_000, vmem=52,
        )
        b3_far = far_swap(b3_own)
        b1g_far = core_swap(b1g)
        dw_cross = (dw_cross[0].astype(F32) + core_swap(dw_cross[1]).astype(F32)).astype(BF16)

        part_grad, dw_self = run(
            self_back,
            [((2, half, model), BF16), ((4, width, model), BF16)],
            place, [b1g, b1g_far, att, h1, qa, ka, va, q_weight, k_weight, v_weight, o_weight],
            scratch=[((count, model), BF16), ((heads, count, 2 * HEAD), BF16), ((heads, count, 2 * HEAD), F32)]
            + [((count, width), BF16)] * 3,
            flops=20_000_000_000, vmem=52,
        )
        h1g_own = (part_grad[0].astype(F32) + core_swap(part_grad[1]).astype(F32)).astype(BF16)
        h1g_far = far_swap(h1g_own)

        mixed, sums_mixed = run(
            mixed_kernel, [((half, model), BF16), ((2, 1, model), F32)],
            place, [mod, cotangent, x1, b2, b3_own, b3_far], flops=10_000_000,
        )
        token_grad, slot_sums = run(
            final_kernel, [((half, model), BF16), ((slots, 9 * model), F32)],
            place, [mod, tokens, h1g_own, h1g_far, x1g, sums_cross, sums_mixed], flops=10_000_000,
        )
        mixed = pair_up(core, mixed, core_swap(mixed))
        token_grad = pair_up(core, token_grad, core_swap(token_grad))

        slot_sums = slot_sums + core_swap(slot_sums)
        local_cols = mod_weight.shape[1]
        slot_grad = lax.dynamic_slice_in_dim(slot_sums, tensor_at * local_cols, local_cols, 1).astype(BF16)
        gathered = jnp.concatenate([silu_low, slot_grad], axis=1)
        for bit in range(dp_bits):
            gathered = jnp.concatenate([gathered, dp_swap(gathered, bit)], axis=0)
        mod_weight_grad = dot_tn(gathered[:, :model], gathered[:, model:])
        mod_bias_grad = jnp.sum(gathered[:, model:].astype(F32), axis=0)

        def dp_sum(keep, send):
            total = (keep.astype(F32) + dp_swap(send, 0).astype(F32)).astype(BF16)
            for bit in range(1, dp_bits):
                flag = (dp_at >> bit) & 1
                size = total.shape[0] // 2
                keep = lax.dynamic_slice_in_dim(total, flag * size, size, 0)
                send = lax.dynamic_slice_in_dim(total, (1 - flag) * size, size, 0)
                total = (keep.astype(F32) + dp_swap(send, bit).astype(F32)).astype(BF16)
            for bit in reversed(range(1, dp_bits)):
                total = pair_up((dp_at >> bit) & 1, total, dp_swap(total, bit))
            other = dp_swap(total, 0)
            first = jnp.where(row == 0, total, other).astype(F32)
            second = jnp.where(row == 0, other, total).astype(F32)
            return first, second

        mlp_in_grad, mlp_out_grad = dp_sum(dw_mlp[0], dw_mlp[1])
        flat = (2, 2 * width, model)
        dw_cross = dw_cross.reshape(flat)
        dw_self = dw_self.reshape(flat)
        cross_qk, cross_vo = dp_sum(dw_cross[0], dw_cross[1])
        self_qk, self_vo = dp_sum(dw_self[0], dw_self[1])
        return (
            mixed,
            token_grad,
            self_qk[:width].T,
            self_qk[width:].T,
            self_vo[:width].T,
            self_vo[width:],
            cross_qk[:width].T,
            cross_qk[width:].T,
            cross_vo[:width].T,
            cross_vo[width:],
            mlp_in_grad,
            mlp_out_grad,
            mod_weight_grad,
            mod_bias_grad,
        )

    rows = P("dp", None)
    by_col = P(None, "tensor")
    by_row = P("tensor", None)
    return jax.shard_map(
        local,
        mesh=mesh,
        in_specs=(
            rows, P("dp", None, None), P("dp"), P("dp"), P("dp"), by_col, by_col, by_col, by_row,
            by_col, by_col, by_col, by_row, by_col, by_row, by_col, P("tensor"), rows,
        ),
        out_specs=(
            rows, rows, by_col, by_col, by_col, by_row, by_col, by_col, by_col, by_row,
            by_col, by_row, by_col, P("tensor"),
        ),
        check_vma=False,
    )
```

time: 680 us -> 303 us (0.45); the launches traced: 670 us -> 302 us
  waiting for transfers between devices: 405 us -> 139 us
  matrix products: 128 us -> 4.07 us
  Pallas kernels: 0 us -> 76 us
  other arithmetic: 62 us -> 13.7 us
  starting transfers between devices: 1.21 us -> 39.7 us
  blocking collectives: 28.9 us -> 0 us
  between operations: 15.9 us -> 1.37 us
    psum x6 -> x0, waiting for transfers between devices: 405 us -> none  [the longest x1 210 us: local(): lax.psum(q_weight_grad.astype(jnp.bfloat16), 'dp').astype(jnp.float32)]
    ppermute x0 -> x41, waiting for transfers between devices: none -> 139 us  [the longest x21 101 us: dp_swap(): return lax.ppermute(value, 'dp', [(i, i ^ 1 << bit) for i in range(n_dp)])]
    dot_general x72 -> x2, matrix products: 128 us -> 4.07 us  [the longest x1 3.29 us: dot_tn(): lax.dot_general(a, b, (((0,), (0,)), ((), ())), preferred_element_type=F32)]
    pallas_call x0 -> x7, Pallas kernels: none -> 76 us  [run(): pl.pallas_call(kernel, out_shape=[jax.ShapeDtypeStruct(shape, kind) for s...]
    ppermute x0 -> x41, starting transfers between devices: none -> 39.7 us  [the longest x21 29.3 us: dp_swap(): return lax.ppermute(value, 'dp', [(i, i ^ 1 << bit) for i in range(n_dp)])]
    convert_element_type x22 -> x20, other arithmetic: 41.5 us -> 8.83 us  [the longest x3 2.91 us: dp_sum(): second = jnp.where(row == 0, other, total).astype(F32)]
    psum x1 -> x0, blocking collectives: 22.4 us -> none  [local(): lax.psum(mod_bias_grad.astype(jnp.bfloat16), 'dp').astype(jnp.float32)]
    reduce_sum x13 -> x2, other arithmetic: 16.1 us -> 0.83 us  [the longest x1 0.65 us: local(): mod_bias_grad = jnp.sum(gathered[:, model:].astype(F32), axis=0)]
  transfers between devices with their start and end apart: 6 -> 41, of which waited for: 6 -> 16; matrix products, arithmetic and copies ran while one was open for 9% -> 10% of each run, Pallas kernels for 0% -> 18%
where the time goes in v1:
time: 303 us; the launch traced here: 302 us
  waiting for transfers between devices  139 us (46%)
  Pallas kernels  76 us (25%)
  starting transfers between devices  39.7 us (13%)
  local copies, waits for them, and re-layouts  28.7 us (9%)
  other arithmetic  13.7 us (5%)
  matrix products  4.07 us (1%)
    ppermute x21, waiting for transfers between devices, dp_swap(): return lax.ppermute(value, 'dp', [(i, i ^ 1 << bit) for i in range(n_dp)])  101 us
    pallas_call x7, Pallas kernels, run(): pl.pallas_call(kernel, out_shape=[jax.ShapeDtypeStruct(shape, kind) for s...  76 us
    ppermute x5, waiting for transfers between devices, far_swap(): return lax.ppermute(value, 'tensor', far_pairs)  32.6 us
    ppermute x21, starting transfers between devices, dp_swap(): return lax.ppermute(value, 'dp', [(i, i ^ 1 << bit) for i in range(n_dp)])  29.3 us
    unnamed x93, local copies, waits for them, and re-layouts  16.3 us
  transfers between devices with their start and end apart: 41, of which 16 were waited for; matrix products, arithmetic and copies ran while one was open for 10% of the time, Pallas kernels for 18%

profile of v1, /device:TPU:0, one launch (start us, length us, event | category | flops | bytes accessed | tf_op | source)
XLA Modules:
  0.0 302.2 jit_solution(4454918241709885628)
XLA Ops:
  3.7 2.6 collective-permute-start.1
  19.9 11.4 %shard_map.281 = (bf16[2,512,768]{2,1,0:T(8,128)(2,1)S(1)}, bf16[1024,768]{1,0:T(8,128)(2,1)S(1)}, bf16[3,1024,128]{2,1,0:T(8,128)(2,1)S(1)}, bf16[3,1024,128]{2...) custom-call(s32[12]{0:T(128)S(1)} %concatenate.47.place, ...), custom_call_target="tpu_custom_call" | custom-call | flops 12000000000 | bytes 8000000 | tf_op jit(solution)/shard_map/pallas_call | solution.py:62
  35.9 5.3 %collective-permute-done.5.p1 = bf16[544,768]{1,0:T(8,128)(2,1)S(1)} collective-permute-done((bf16[544,768]{1,0:T(8,128)(2,1)S(1)}, bf16[544,768]{1,0:T(8,128)(2,1)S(1)}, u32[]{:S(2)}, u32[]{:S(2)}) %collective-permute-start.5) | collective-permute-done | bytes 835616 | tf_op jit(solution)/shard_map/ppermute | solution.py:450
  41.2 13.9 %collective-permute-done.4.sum_far = bf16[512,768]{1,0:T(8,128)(2,1)S(1)} collective-permute-done((bf16[512,768]{1,0:T(8,128)(2,1)S(1)}, bf16[512,768]{1,0:T(8,128)(2,1)S(1)}, u32[]{:S(2)}, u32[]{:S(2)}) %collective-permute-start.4) | collective-permute-done | bytes 786464 | tf_op jit(solution)/shard_map/ppermute | solution.py:453
  56.9 21.3 %shard_map.283 = (f32[512,768]{1,0:T(8,128)}, f32[512,768]{1,0:T(8,128)}, bf16[512,768]{1,0:T(8,128)(2,1)S(1)}, bf16[512,768]{1,0:T(8,128)(2,1)}, bf16[512,768]{...) custom-call(s32[12]{0:T(128)S(1)} %concatenate.47.place, ...), custom_call_target="tpu_custom_call" | custom-call | flops 16000000000 | bytes 8000000 | tf_op jit(solution)/shard_map/pallas_call | solution.py:62
  81.2 18.7 %collective-permute-done.12.h3g_far = bf16[512,768]{1,0:T(8,128)(2,1)S(1)} collective-permute-done((bf16[512,768]{1,0:T(8,128)(2,1)}, bf16[512,768]{1,0:T(8,128)(2,1)S(1)}, u32[]{:S(2)}, u32[]{:S(2)}) %collective-permute-start.12) | collective-permute-done | bytes 786464 | tf_op jit(solution)/shard_map/ppermute | solution.py:453
  100.7 19.2 %shard_map.285 = (bf16[512,768]{1,0:T(8,128)(2,1)}, f32[512,768]{1,0:T(8,128)}, bf16[2,4,192,768]{3,2,1,0:T(8,128)(2,1)}, f32[2,8,768]{2,1,0:T(8,128)S(1)}) custom-call(s32[12]{0:T(128)S(1)} %concatenate.47.place, f32[4,6912]{1,0:T(4,128)S(1)} %concatenate.49.mod, bf16[1024,768]{1,0:T(8,128)(2,1)} %cot.5, bf16[4,80,768]{2,1,0:T(8,128)(2,1)S(1)} %pad.4.text, ...), custom_call_target="tpu_custom_call" | custom-call | flops 8000000000 | bytes 8000000 | tf_op jit(solution)/shard_map/pallas_call | solution.py:62
  120.0 3.4 %slice_bitcast_fusion = bf16[2,768,768]{2,1,0:T(8,128)(2,1)} fusion(bf16[2,2,768,768]{3,2,1,0:T(8,128)(2,1)} %get-tuple-element.64), kind=kLoop, calls=%fused_computation.6 | loop fusion | bytes 4718592 | tf_op jit(solution)/shard_map/squeeze | solution.py:530
  123.8 2.6 slice_bitcast_fusion.3
  128.2 19.7 %shard_map.286 = (bf16[2,512,768]{2,1,0:T(8,128)(2,1)}, bf16[4,192,768]{2,1,0:T(8,128)(2,1)}) custom-call(s32[12]{0:T(128)S(1)} %concatenate.47.place, bf16[512,768]{1,0:T(8,128)(2,1)} %get-tuple-element.51.b1g_own, bf16[512,768]{1,0:T(8,128)(2,1)} %collective-permute-done.13.b1g_far, bf16[1024,192]{1,0:T(8,128)(2,1)S(1)} %copy-done.23, ...), custom_call_target="tpu_custom_call" | custom-call | flops 20000000000 | bytes 8000000 | tf_op jit(solution)/shard_map/pallas_call | solution.py:62
  155.1 10.6 %collective-permute-done.17 = bf16[384,768]{1,0:T(8,128)(2,1)S(1)} collective-permute-done((bf16[384,768]{1,0:T(8,128)(2,1)S(1)}, bf16[384,768]{1,0:T(8,128)(2,1)S(1)}, u32[]{:S(2)}, u32[]{:S(2)}) %collective-permute-start.17) | collective-permute-done | bytes 589856 | tf_op jit(solution)/shard_map/ppermute | solution.py:456
  169.0 4.8 %collective-permute-done.18 = bf16[192,768]{1,0:T(8,128)(2,1)S(1)} collective-permute-done((bf16[192,768]{1,0:T(8,128)(2,1)S(1)}, bf16[192,768]{1,0:T(8,128)(2,1)S(1)}, u32[]{:S(2)}, u32[]{:S(2)}) %collective-permute-start.18) | collective-permute-done | bytes 294944 | tf_op jit(solution)/shard_map/ppermute | solution.py:456
  174.0 2.6 collective-permute-start.19
  184.0 6.4 %collective-permute-done.25 = bf16[192,768]{1,0:T(8,128)(2,1)S(1)} collective-permute-done((bf16[192,768]{1,0:T(8,128)(2,1)S(1)}, bf16[192,768]{1,0:T(8,128)(2,1)S(1)}, u32[]{:S(2)}, u32[]{:S(2)}) %collective-permute-start.25) | collective-permute-done | bytes 294944 | tf_op jit(solution)/shard_map/ppermute | solution.py:456
  190.5 2.6 collective-permute-start.26
  193.2 2.5 collective-permute-start.21
  202.1 5.0 %collective-permute-done.31 = bf16[768,768]{1,0:T(8,128)(2,1)S(1)} collective-permute-done((bf16[768,768]{1,0:T(8,128)(2,1)S(1)}, bf16[768,768]{1,0:T(8,128)(2,1)S(1)}, u32[]{:S(2)}, u32[]{:S(2)}) %collective-permute-start.31) | collective-permute-done | bytes 1179680 | tf_op jit(solution)/shard_map/ppermute | solution.py:456
  209.7 12.9 %collective-permute-done.39 = bf16[8,2496]{1,0:T(8,128)(2,1)S(1)} collective-permute-done((bf16[8,2496]{1,0:T(8,128)(2,1)S(1)}, bf16[8,2496]{1,0:T(8,128)(2,1)S(1)}, u32[]{:S(2)}, u32[]{:S(2)}) %collective-permute-start.39) | collective-permute-done | bytes 39968 | tf_op jit(solution)/shard_map/ppermute | solution.py:456
  227.7 8.3 %collective-permute-done.40 = bf16[16,2496]{1,0:T(8,128)(2,1)S(1)} collective-permute-done((bf16[16,2496]{1,0:T(8,128)(2,1)S(1)}, bf16[16,2496]{1,0:T(8,128)(2,1)S(1)}, u32[]{:S(2)}, u32[]{:S(2)}) %collective-permute-start.40) | collective-permute-done | bytes 79904 | tf_op jit(solution)/shard_map/ppermute | solution.py:456
  236.1 3.3 %fusion.7 = f32[768,1728]{0,1:T(8,128)} fusion(bf16[16,2496]{1,0:T(8,128)(2,1)S(1)} %collective-permute-done.40, bf16[8,2496]{1,0:T(8,128)(2,1)S(1)} %collective-permute-done.39, bf16[4,2496]{1,0:T(4,128)(2,1)S(1)} %collective-permute-done.38, bf16[4,1728]{1,0:T(4,128)(2,1)S(1)} %fusion.17, bf16[4,768]{1,0:T(4,128)(2,1)S(1)} %fusion.18), kind=kOutput, calls=%fused_computation.70 | convolution fusion | flops 85733376 | bytes 5468160 | tf_op jit(solution)/shard_map/dot_general | solution.py:29
  245.1 12.9 %collective-permute-done.34 = bf16[192,768]{1,0:T(8,128)(2,1)S(1)} collective-permute-done((bf16[192,768]{1,0:T(8,128)(2,1)S(1)}, bf16[192,768]{1,0:T(8,128)(2,1)S(1)}, u32[]{:S(2)}, u32[]{:S(2)}) %collective-permute-start.34) | collective-permute-done | bytes 294944 | tf_op jit(solution)/shard_map/ppermute | solution.py:456
  259.9 12.9 %collective-permute-done.35 = bf16[384,768]{1,0:T(8,128)(2,1)S(1)} collective-permute-done((bf16[384,768]{1,0:T(8,128)(2,1)S(1)}, bf16[384,768]{1,0:T(8,128)(2,1)S(1)}, u32[]{:S(2)}, u32[]{:S(2)}) %collective-permute-start.35) | collective-permute-done | bytes 589856 | tf_op jit(solution)/shard_map/ppermute | solution.py:456
  279.2 20.2 %collective-permute-done.36 = bf16[768,768]{1,0:T(8,128)(2,1)S(1)} collective-permute-done((bf16[768,768]{1,0:T(8,128)(2,1)S(1)}, bf16[768,768]{1,0:T(8,128)(2,1)S(1)}, u32[]{:S(2)}, u32[]{:S(2)}) %collective-permute-start.36) | collective-permute-done | bytes 1179680 | tf_op jit(solution)/shard_map/ppermute | solution.py:456
  299.4 2.6 select_convert_fusion
  (228 shorter events, 75.2 us)
Async XLA Ops:
  9.9 25.0 %collective-permute-start.6 = (bf16[544,768]{1,0:T(8,128)(2,1)S(1)}, bf16[544,768]{1,0:T(8,128)(2,1)}, u32[]{:S(2)}, u32[]{:S(2)}) collective-permute-start(bf16[544,768]{1,0:T(8,128)(2,1)S(1)} %shard_map.282.p0), channel_id=1, source_target_pairs={{0,2},{1,3},{2,0},{3,1},{4,6},{5,7},{6,4},{7,5},{8,10},{9,11},{10,... | collective-permute-start | bytes 2506760 | tf_op jit(solution)/shard_map/ppermute | solution.py:453
  34.8 20.3 %collective-permute-start.7 = (bf16[544,768]{1,0:T(8,128)(2,1)}, bf16[544,768]{1,0:T(8,128)(2,1)S(1)}, u32[]{:S(2)}, u32[]{:S(2)}) collective-permute-start(bf16[544,768]{1,0:T(8,128)(2,1)} %collective-permute-done.6.p2), channel_id=1, source_target_pairs={{0,1},{1,0},{2,3},{3,2},{4,5},{5,4},{6,7},{7,6},{8,9},{9,8},{10,11... | collective-permute-start | bytes 2506760 | tf_op jit(solution)/shard_map/ppermute | solution.py:450
  35.5 19.6 %collective-permute-start.4 = (bf16[512,768]{1,0:T(8,128)(2,1)S(1)}, bf16[512,768]{1,0:T(8,128)(2,1)S(1)}, u32[]{:S(2)}, u32[]{:S(2)}) collective-permute-start(bf16[512,768]{1,0:T(8,128)(2,1)S(1)} %fusion.4.sum_own), channel_id=1, source_target_pairs={{0,2},{1,3},{2,0},{3,1},{4,6},{5,7},{6,4},{7,5},{8,10},{9,11},{10,... | collective-permute-start | bytes 2359304 | tf_op jit(solution)/shard_map/ppermute | solution.py:453
  79.2 20.7 %collective-permute-start.12 = (bf16[512,768]{1,0:T(8,128)(2,1)}, bf16[512,768]{1,0:T(8,128)(2,1)S(1)}, u32[]{:S(2)}, u32[]{:S(2)}) collective-permute-start(bf16[512,768]{1,0:T(8,128)(2,1)} %get-tuple-element.45.h3g_own), channel_id=1, source_target_pairs={{0,2},{1,3},{2,0},{3,1},{4,6},{5,7},{6,4},{7,5},{8,10},{9,11},{10,... | collective-permute-start | bytes 2359304 | tf_op jit(solution)/shard_map/ppermute | solution.py:453
  79.7 46.8 %collective-permute-start.10 = (bf16[512,768]{1,0:T(8,128)(2,1)}, bf16[512,768]{1,0:T(8,128)(2,1)S(1)}, u32[]{:S(2)}, u32[]{:S(2)}) collective-permute-start(bf16[512,768]{1,0:T(8,128)(2,1)} %get-tuple-element.43.b3_own), channel_id=1, source_target_pairs={{0,2},{1,3},{2,0},{3,1},{4,6},{5,7},{6,4},{7,5},{8,10},{9,11},{10,... | collective-permute-start | bytes 2359304 | tf_op jit(solution)/shard_map/ppermute | solution.py:453
  123.3 45.1 %collective-permute-start.30 = (bf16[2,768,768]{2,1,0:T(8,128)(2,1)}, bf16[2,768,768]{2,1,0:T(8,128)(2,1)S(1)}, u32[]{:S(2)}, u32[]{:S(2)}) collective-permute-start(bf16[2,768,768]{2,1,0:T(8,128)(2,1)} %slice_bitcast_fusion), channel_id=1, source_target_pairs={{0,1},{1,0},{2,3},{3,2},{4,5},{5,4},{6,7},{7,6},{8,9},{9,8},{10,11... | collective-permute-start | bytes 7077896 | tf_op jit(solution)/shard_map/ppermute | solution.py:450
  126.4 26.1 %collective-permute-start.23 = (bf16[4,192,768]{2,1,0:T(8,128)(2,1)}, bf16[4,192,768]{2,1,0:T(8,128)(2,1)}, u32[]{:S(2)}, u32[]{:S(2)}) collective-permute-start(bf16[4,192,768]{2,1,0:T(8,128)(2,1)} %slice_bitcast_fusion.3), channel_id=1, source_target_pairs={{0,1},{1,0},{2,3},{3,2},{4,5},{5,4},{6,7},{7,6},{8,9},{9,8},{10,11... | collective-permute-start | bytes 3538952 | tf_op jit(solution)/shard_map/ppermute | solution.py:450
  127.6 23.4 %collective-permute-start.11 = (bf16[512,768]{1,0:T(8,128)(2,1)S(1)}, bf16[512,768]{1,0:T(8,128)(2,1)S(1)}, u32[]{:S(2)}, u32[]{:S(2)}) collective-permute-start(bf16[512,768]{1,0:T(8,128)(2,1)S(1)} %get-tuple-element.44), channel_id=1, source_target_pairs={{0,1},{1,0},{2,3},{3,2},{4,5},{5,4},{6,7},{7,6},{8,9},{9,8},{10,11... | collective-permute-start | bytes 2359304 | tf_op jit(solution)/shard_map/ppermute | solution.py:450
  149.1 18.4 %collective-permute-start.14 = (bf16[512,768]{1,0:T(8,128)(2,1)S(1)}, bf16[512,768]{1,0:T(8,128)(2,1)S(1)}, u32[]{:S(2)}, u32[]{:S(2)}) collective-permute-start(bf16[512,768]{1,0:T(8,128)(2,1)S(1)} %slice_bitcast_fusion.4), channel_id=1, source_target_pairs={{0,1},{1,0},{2,3},{3,2},{4,5},{5,4},{6,7},{7,6},{8,9},{9,8},{10,11... | collective-permute-start | bytes 2359304 | tf_op jit(solution)/shard_map/ppermute | solution.py:450
  149.5 16.2 %collective-permute-start.17 = (bf16[384,768]{1,0:T(8,128)(2,1)S(1)}, bf16[384,768]{1,0:T(8,128)(2,1)S(1)}, u32[]{:S(2)}, u32[]{:S(2)}) collective-permute-start(bf16[384,768]{1,0:T(8,128)(2,1)S(1)} %bitcast.68), channel_id=1, source_target_pairs={{0,4},{4,0},{8,12},{12,8},{16,20},{20,16},{24,28},{28,24},{1,5},{5... | collective-permute-start | bytes 1769480 | tf_op jit(solution)/shard_map/ppermute | solution.py:456
  154.6 23.2 %collective-permute-start.24 = (bf16[384,768]{1,0:T(8,128)(2,1)S(1)}, bf16[384,768]{1,0:T(8,128)(2,1)S(1)}, u32[]{:S(2)}, u32[]{:S(2)}) collective-permute-start(bf16[384,768]{1,0:T(8,128)(2,1)S(1)} %bitcast.67), channel_id=1, source_target_pairs={{0,4},{4,0},{8,12},{12,8},{16,20},{20,16},{24,28},{28,24},{1,5},{5... | collective-permute-start | bytes 1769480 | tf_op jit(solution)/shard_map/ppermute | solution.py:456
  167.8 28.0 %collective-permute-start.15 = (bf16[512,768]{1,0:T(8,128)(2,1)S(1)}, bf16[512,768]{1,0:T(8,128)(2,1)S(1)}, u32[]{:S(2)}, u32[]{:S(2)}) collective-permute-start(bf16[512,768]{1,0:T(8,128)(2,1)S(1)} %fusion.3.h1g_own), channel_id=1, source_target_pairs={{0,2},{1,3},{2,0},{3,1},{4,6},{5,7},{6,4},{7,5},{8,10},{9,11},{10,... | collective-permute-start | bytes 2359304 | tf_op jit(solution)/shard_map/ppermute | solution.py:453
  179.7 27.4 %collective-permute-start.31 = (bf16[768,768]{1,0:T(8,128)(2,1)S(1)}, bf16[768,768]{1,0:T(8,128)(2,1)S(1)}, u32[]{:S(2)}, u32[]{:S(2)}) collective-permute-start(bf16[768,768]{1,0:T(8,128)(2,1)S(1)} %slice_bitcast_fusion.1), channel_id=1, source_target_pairs={{0,4},{4,0},{8,12},{12,8},{16,20},{20,16},{24,28},{28,24},{1,5},{5... | collective-permute-start | bytes 3538952 | tf_op jit(solution)/shard_map/ppermute | solution.py:456
  193.2 49.5 %collective-permute-start.21 = (bf16[192,768]{1,0:T(8,128)(2,1)S(1)}, bf16[192,768]{1,0:T(8,128)(2,1)S(1)}, u32[]{:S(2)}, u32[]{:S(2)}) collective-permute-start(bf16[192,768]{1,0:T(8,128)(2,1)S(1)} %pad_maximum_fusion.6), channel_id=1, source_target_pairs={{0,8},{4,12},{8,0},{12,4},{16,24},{20,28},{24,16},{28,20},{1,9},{5... | collective-permute-start | bytes 884744 | tf_op jit(solution)/shard_map/ppermute | solution.py:456
  207.5 17.4 %collective-permute-start.32 = (bf16[384,768]{1,0:T(8,128)(2,1)S(1)}, bf16[384,768]{1,0:T(8,128)(2,1)S(1)}, u32[]{:S(2)}, u32[]{:S(2)}) collective-permute-start(bf16[384,768]{1,0:T(8,128)(2,1)S(1)} %constant_dynamic-slice_fusion.1), channel_id=1, source_target_pairs={{0,8},{4,12},{8,0},{12,4},{16,24},{20,28},{24,16},{28,20},{1,9},{5... | collective-permute-start | bytes 1769480 | tf_op jit(solution)/shard_map/ppermute | solution.py:456
  208.0 14.6 %collective-permute-start.39 = (bf16[8,2496]{1,0:T(8,128)(2,1)S(1)}, bf16[8,2496]{1,0:T(8,128)(2,1)S(1)}, u32[]{:S(2)}, u32[]{:S(2)}) collective-permute-start(bf16[8,2496]{1,0:T(8,128)(2,1)S(1)} %pad_maximum_fusion.14), channel_id=1, source_target_pairs={{0,8},{4,12},{8,0},{12,4},{16,24},{20,28},{24,16},{28,20},{1,9},{5... | collective-permute-start | bytes 119816 | tf_op jit(solution)/shard_map/ppermute | solution.py:456
  225.1 17.4 %collective-permute-start.33 = (bf16[192,768]{1,0:T(8,128)(2,1)S(1)}, bf16[192,768]{1,0:T(8,128)(2,1)S(1)}, u32[]{:S(2)}, u32[]{:S(2)}) collective-permute-start(bf16[192,768]{1,0:T(8,128)(2,1)S(1)} %constant_dynamic-slice_fusion), channel_id=1, source_target_pairs={{0,16},{4,20},{8,24},{12,28},{16,0},{20,4},{24,8},{28,12},{1,17},{... | collective-permute-start | bytes 884744 | tf_op jit(solution)/shard_map/ppermute | solution.py:456
  226.0 16.7 %collective-permute-start.28 = (bf16[192,768]{1,0:T(8,128)(2,1)S(1)}, bf16[192,768]{1,0:T(8,128)(2,1)S(1)}, u32[]{:S(2)}, u32[]{:S(2)}) collective-permute-start(bf16[192,768]{1,0:T(8,128)(2,1)S(1)} %pad_maximum_fusion.7), channel_id=1, source_target_pairs={{0,8},{4,12},{8,0},{12,4},{16,24},{20,28},{24,16},{28,20},{1,9},{5... | collective-permute-start | bytes 884744 | tf_op jit(solution)/shard_map/ppermute | solution.py:456
  227.7 30.5 %collective-permute-start.16 = (bf16[512,768]{1,0:T(8,128)(2,1)S(1)}, bf16[512,768]{1,0:T(8,128)(2,1)S(1)}, u32[]{:S(2)}, u32[]{:S(2)}) collective-permute-start(bf16[512,768]{1,0:T(8,128)(2,1)S(1)} %get-tuple-element.61), channel_id=1, source_target_pairs={{0,1},{1,0},{2,3},{3,2},{4,5},{5,4},{6,7},{7,6},{8,9},{9,8},{10,11... | collective-permute-start | bytes 2359304 | tf_op jit(solution)/shard_map/ppermute | solution.py:450
  242.6 15.5 %collective-permute-start.34 = (bf16[192,768]{1,0:T(8,128)(2,1)S(1)}, bf16[192,768]{1,0:T(8,128)(2,1)S(1)}, u32[]{:S(2)}, u32[]{:S(2)}) collective-permute-start(bf16[192,768]{1,0:T(8,128)(2,1)S(1)} %add_convert_fusion.1), channel_id=1, source_target_pairs={{0,16},{4,20},{8,24},{12,28},{16,0},{20,4},{24,8},{28,12},{1,17},{... | collective-permute-start | bytes 884744 | tf_op jit(solution)/shard_map/ppermute | solution.py:456
  242.9 16.8 %collective-permute-start.29 = (bf16[384,768]{1,0:T(8,128)(2,1)S(1)}, bf16[384,768]{1,0:T(8,128)(2,1)S(1)}, u32[]{:S(2)}, u32[]{:S(2)}) collective-permute-start(bf16[384,768]{1,0:T(8,128)(2,1)S(1)} %pad_maximum_fusion.4), channel_id=1, source_target_pairs={{0,4},{4,0},{8,12},{12,8},{16,20},{20,16},{24,28},{28,24},{1,5},{5... | collective-permute-start | bytes 1769480 | tf_op jit(solution)/shard_map/ppermute | solution.py:456
  244.6 32.3 %collective-permute-start.22 = (bf16[384,768]{1,0:T(8,128)(2,1)S(1)}, bf16[384,768]{1,0:T(8,128)(2,1)S(1)}, u32[]{:S(2)}, u32[]{:S(2)}) collective-permute-start(bf16[384,768]{1,0:T(8,128)(2,1)S(1)} %pad_maximum_fusion.3), channel_id=1, source_target_pairs={{0,4},{4,0},{8,12},{12,8},{16,20},{20,16},{24,28},{28,24},{1,5},{5... | collective-permute-start | bytes 1769480 | tf_op jit(solution)/shard_map/ppermute | solution.py:456
  258.2 14.6 %collective-permute-start.35 = (bf16[384,768]{1,0:T(8,128)(2,1)S(1)}, bf16[384,768]{1,0:T(8,128)(2,1)S(1)}, u32[]{:S(2)}, u32[]{:S(2)}) collective-permute-start(bf16[384,768]{1,0:T(8,128)(2,1)S(1)} %pad_maximum_fusion.5), channel_id=1, source_target_pairs={{0,8},{4,12},{8,0},{12,4},{16,24},{20,28},{24,16},{28,20},{1,9},{5... | collective-permute-start | bytes 1769480 | tf_op jit(solution)/shard_map/ppermute | solution.py:456
  273.1 26.3 %collective-permute-start.36 = (bf16[768,768]{1,0:T(8,128)(2,1)S(1)}, bf16[768,768]{1,0:T(8,128)(2,1)S(1)}, u32[]{:S(2)}, u32[]{:S(2)}) collective-permute-start(bf16[768,768]{1,0:T(8,128)(2,1)S(1)} %pad_maximum_fusion.2), channel_id=1, source_target_pairs={{0,4},{4,0},{8,12},{12,8},{16,20},{20,16},{24,28},{28,24},{1,5},{5... | collective-permute-start | bytes 3538952 | tf_op jit(solution)/shard_map/ppermute | solution.py:456
  (60 other events, 396.9 us)
